TPU v7x, 512 devices: a whole 4x8x8 slice. The times are simulated.
512 devices in a mesh: wide: 64 (over y, z), narrow: 8 (over x, core).
Axes of the slice: x: 4, y: 8, z: 8, core: 2. Of those that a mesh axis runs over, the one named last changes fastest.
Arguments:
- amplitudes: bfloat16 [262144, 512], P('narrow', 'wide'), may hold values from -6 to 6
- integrals: bfloat16 [8, 64, 512, 1536], P('narrow', 'wide'), may hold values from -0.15625 to 0.15625
- amplitude_mask: int32 [4096, 64], P('narrow', 'wide'), may hold values 0 or 1
- integral_mask: int32 [8, 64, 8, 24], P('narrow', 'wide'), may hold values from 0 to 1
Outputs:
- residual: float32 [32768, 512], P(('narrow', 'wide'))
All inputs are finite; a program needn't handle non-finite values. No bound on the sum of `amplitude_mask` on one device may be relied on, other than what follows from the above.
Results may differ from a plain program's by a relative error of at most 0.0003.
Values may be sent and summed in bfloat16 or wider, within the bound.
A program may use at most 64 MiB of HBM per device.

v0:
```python
import jax
import jax.numpy as jnp
from jax import lax
from jax.sharding import PartitionSpec as P

TILE = 64


def with_halo(cells, sides, width):
    for axis, dim in sides:
        count = lax.axis_size(axis)
        ends = count - 1
        head = lax.slice_in_dim(cells, 0, width, axis=dim)
        tail = lax.slice_in_dim(cells, cells.shape[dim] - width, cells.shape[dim], axis=dim)
        cells = jnp.concatenate(
            [
                lax.ppermute(tail, axis, [(i, (i + 1) % count) for i in range(ends)]),
                cells,
                lax.ppermute(head, axis, [((i + 1) % count, i) for i in range(ends)]),
            ],
            axis=dim,
        )
    return cells


def body(amplitudes, integrals, amplitude_mask, integral_mask):
    columns = amplitudes.shape[1]
    block_pairs = integrals.shape[3] // 3
    tile_mask = jnp.repeat(jnp.repeat(amplitude_mask, TILE, axis=0), columns, axis=1).astype(
        jnp.bfloat16
    )
    masked = amplitudes * tile_mask
    owned = lax.all_to_all(masked, "wide", split_axis=0, concat_axis=1, tiled=True)
    nearby = with_halo(owned, (("wide", 0),), block_pairs)
    flags = integral_mask[0, 0]
    wide_flags = jnp.repeat(jnp.repeat(flags, TILE, axis=0), TILE, axis=1).astype(jnp.bfloat16)
    weights = integrals[0, 0] * wide_flags
    return lax.psum_scatter(
        jnp.dot(weights, nearby, preferred_element_type=jnp.float32),
        "narrow",
        scatter_dimension=0,
        tiled=True,
    )


def solution(mesh):
    return jax.shard_map(
        body,
        mesh=mesh,
        in_specs=(
            P("narrow", "wide"),
            P("narrow", "wide", None, None),
            P("narrow", "wide"),
            P("narrow", "wide", None, None),
        ),
        out_specs=P(("narrow", "wide"), None),
        check_vma=False,
    )
```

profile of v0, /device:TPU:8, one launch (start us, length us, event | category | flops | bytes accessed | tf_op | source)
XLA Modules:
  0.0 107.2 jit_solution(11526608389456543400)
XLA Ops:
  6.5 0.0 copy-start.1
  6.5 0.0 copy-start
  6.5 0.0 reduce-scatter.2.cloned.1.call-start
  6.5 0.8 convert_reduce_fusion
  7.4 0.1 broadcast_in_dim.12
  7.5 0.1 convert_element_type.31
  7.6 1.1 %broadcast_multiply_fusion = bf16[32768,8]{0,1:T(8,128)(2,1)S(1)} fusion(bf16[32768,8]{0,1:T(8,128)(2,1)} %param.4, bf16[32768]{0:T(1024)(128)(2,1)S(1)} %convert_element_type.31), kind=kLoop, calls=%fused_computation.7 | loop fusion | flops 262144 | bytes 1114112 | tf_op jit(solution)/shard_map/mul | solution.py:32
  8.7 35.0 %all_to_all.19 = bf16[64,512,8]{1,2,0:T(8,128)(2,1)} all-to-all(bf16[64,512,8]{1,2,0:T(8,128)(2,1)S(1)} %bitcast.13), channel_id=1, replica_groups=mesh['wide'=64,'narrow'=8] {'wide'}, dimensions={0} | all-to-all | bytes 1048576 | tf_op jit(solution)/shard_map/all_to_all | solution.py:33
  43.8 3.3 %collective-permute-start.1 = (bf16[512,512]{0,1:T(8,128)(2,1)}, bf16[512,512]{0,1:T(8,128)(2,1)}, u32[]{:S(2)}, u32[]{:S(2)}) collective-permute-start(bf16[512,512]{0,1:T(8,128)(2,1)} %bitcast.5), channel_id=1, source_target_pairs={{8,0},{16,8},{24,16},{32,24},{40,32},{48,40},{56,48},{64,56},{72,6... | collective-permute-start | bytes 1572872 | tf_op jit(solution)/shard_map/ppermute | solution.py:19
  47.1 2.6 %collective-permute-start = (bf16[512,512]{0,1:T(8,128)(2,1)}, bf16[512,512]{0,1:T(8,128)(2,1)}, u32[]{:S(2)}, u32[]{:S(2)}) collective-permute-start(bf16[512,512]{0,1:T(8,128)(2,1)} %bitcast.5), channel_id=1, source_target_pairs={{0,8},{8,16},{16,24},{24,32},{32,40},{40,48},{48,56},{56,64},{64,7... | collective-permute-start | bytes 1572872 | tf_op jit(solution)/shard_map/ppermute | solution.py:17
  49.6 0.0 copy-done.1
  49.6 0.1 copy.6
  49.7 0.1 broadcast_in_dim.10
  49.8 0.1 convert_element_type.27
  49.9 0.0 copy-done
  50.0 0.7 copy.5
  50.7 0.1 bitcast_multiply_fusion
  50.8 6.4 %collective-permute-done.1 = bf16[512,512]{0,1:T(8,128)(2,1)} collective-permute-done((bf16[512,512]{0,1:T(8,128)(2,1)}, bf16[512,512]{0,1:T(8,128)(2,1)}, u32[]{:S(2)}, u32[]{:S(2)}) %collective-permute-start.1) | collective-permute-done | bytes 524320 | tf_op jit(solution)/shard_map/ppermute | solution.py:19
  57.2 5.5 %collective-permute-done = bf16[512,512]{0,1:T(8,128)(2,1)} collective-permute-done((bf16[512,512]{0,1:T(8,128)(2,1)}, bf16[512,512]{0,1:T(8,128)(2,1)}, u32[]{:S(2)}, u32[]{:S(2)}) %collective-permute-start) | collective-permute-done | bytes 524320 | tf_op jit(solution)/shard_map/ppermute | solution.py:17
  62.7 3.4 %fusion = f32[512,512]{1,0:T(8,128)} fusion(bf16[512,1536]{0,1:T(8,128)(2,1)S(1)} %bitcast_multiply_fusion, bf16[512,512]{0,1:T(8,128)(2,1)} %collective-permute-done.1, bf16[512,512]{0,1:T(8,128)(2,1)} %bitcast.5, bf16[512,512]{0,1:T(8,128)(2,1)} %collective-permute-done), kind=kOutput, calls=%fused_computation | convolution fusion | flops 810024960 | bytes 4194304 | tf_op jit(solution)/shard_map/dot_general | solution.py:39
  66.1 0.0 reduce-scatter.2.cloned.1.call-update
  66.1 34.3 %reduce-scatter.2.cloned.1.call-done = f32[64,512]{1,0:T(8,128)} async-done(((f32[512,512]{1,0:T(8,128)}), f32[64,512]{1,0:T(8,128)}) %reduce-scatter.2.cloned.1.call-update) | async-done | bytes 131088 | tf_op jit(solution)/shard_map/reduce_scatter | solution.py:38
  (1 shorter events, 0.0 us)
Async XLA Ops:
  6.5 43.1 %copy-start.1 = (s32[1,1,8,24]{3,2,1,0:T(8,128)S(1)}, s32[1,1,8,24]{3,2,1,0:T(8,128)}, u32[]{:S(2)}) copy-start(s32[1,1,8,24]{3,2,1,0:T(8,128)} %param.7) | copy-start | bytes 2308
  6.5 43.4 %copy-start = (bf16[1,1,512,1536]{3,2,1,0:T(8,128)(2,1)S(1)}, bf16[1,1,512,1536]{3,2,1,0:T(8,128)(2,1)}, u32[]{:S(2)}) copy-start(bf16[1,1,512,1536]{3,2,1,0:T(8,128)(2,1)} %param.5) | copy-start | bytes 4718596
  6.5 93.8 %reduce-scatter.2.cloned.1.call-start = ((), (), s32[]{:S(2)}) async-start(), calls=%async_computation.2 | async-start | bytes 1179648 | tf_op jit(solution)/shard_map/reduce_scatter | solution.py:38
  43.8 13.4 %collective-permute-start.1 = (bf16[512,512]{0,1:T(8,128)(2,1)}, bf16[512,512]{0,1:T(8,128)(2,1)}, u32[]{:S(2)}, u32[]{:S(2)}) collective-permute-start(bf16[512,512]{0,1:T(8,128)(2,1)} %bitcast.5), channel_id=1, source_target_pairs={{8,0},{16,8},{24,16},{32,24},{40,32},{48,40},{56,48},{64,56},{72,6... | collective-permute-start | bytes 1572872 | tf_op jit(solution)/shard_map/ppermute | solution.py:19
  47.1 15.6 %collective-permute-start = (bf16[512,512]{0,1:T(8,128)(2,1)}, bf16[512,512]{0,1:T(8,128)(2,1)}, u32[]{:S(2)}, u32[]{:S(2)}) collective-permute-start(bf16[512,512]{0,1:T(8,128)(2,1)} %bitcast.5), channel_id=1, source_target_pairs={{0,8},{8,16},{16,24},{24,32},{32,40},{40,48},{48,56},{56,64},{64,7... | collective-permute-start | bytes 1572872 | tf_op jit(solution)/shard_map/ppermute | solution.py:17
Sparse Core Ops, SparseCore 0:
  66.2 34.0 reduce-scatter.1
where the time goes:
time: 107 us
  waiting for transfers between devices  46.2 us (43%)
  blocking collectives  35 us (33%)
  between operations  13.5 us (13%)
  starting transfers between devices  5.84 us (5%)
  matrix products  3.36 us (3%)
  other arithmetic  2.05 us (2%)
  local copies, waits for them, and re-layouts  1.24 us (1%)
    all_to_all x1, blocking collectives, body(): lax.all_to_all(masked, 'wide', split_axis=0, concat_axis=1, tiled=True)  35 us
    reduce_scatter x1, waiting for transfers between devices, body(): lax.psum_scatter(jnp.dot(weights, nearby, preferred_element_type=jnp.floa...  34.3 us
    ppermute x1, waiting for transfers between devices, with_halo(): lax.ppermute(head, axis, [((i + 1) % count, i) for i in range(ends)])  6.42 us
    ppermute x1, waiting for transfers between devices, with_halo(): lax.ppermute(tail, axis, [(i, (i + 1) % count) for i in range(ends)])  5.5 us
    dot_general x1, matrix products, body(): jnp.dot(weights, nearby, preferred_element_type=jnp.float32)  3.36 us
    ppermute x1, starting transfers between devices, with_halo(): lax.ppermute(head, axis, [((i + 1) % count, i) for i in range(ends)])  3.28 us
    ppermute x1, starting transfers between devices, with_halo(): lax.ppermute(tail, axis, [(i, (i + 1) % count) for i in range(ends)])  2.56 us
  transfers between devices with their start and end apart: 3, of which 3 were waited for; matrix products, arithmetic and copies ran while one was open for 1% of the time, Pallas kernels for 0%

commit v1 on v0

v1 whole, which is shorter than its diff:
```python
import jax
import jax.numpy as jnp
from jax import lax
from jax.experimental import pallas as pl
from jax.experimental.pallas import tpu as pltpu
from jax.sharding import PartitionSpec as P

MESH = pl.DeviceIdType.MESH
TILE = 64
ROW_ORDER = (0, 1, 7, 2, 6, 3, 5, 4)
NT = (((1,), (1,)), ((), ()))


def kernel(
    amp_hbm, int_hbm, amask_ref, imask_ref, out_ref,
    amp, weights, arow, masked, own, low, high, part, from_x, mine, from_core, total,
    load_sem, self_sem, a2a_send, a2a_recv, halo_send, halo_recv, x_send, x_recv, core_send, core_recv,
):
    me = lax.axis_index("wide")
    nar = lax.axis_index("narrow")
    y, z = me // 8, me % 8
    x, core = nar // 2, nar % 2
    up, down = (me + 1) % 64, (me + 63) % 64

    load_amp = pltpu.make_async_copy(amp_hbm, amp, load_sem.at[0])
    load_int = pltpu.make_async_copy(int_hbm, weights, load_sem.at[1])
    load_amp.start()
    load_int.start()

    barrier = pltpu.get_barrier_semaphore()

    def greet(i, _):
        pl.semaphore_signal(barrier, inc=1, device_id={"wide": (me + i) % 64}, device_id_type=MESH)
        return 0

    lax.fori_loop(1, 64, greet, 0)
    for k in (1, 2, 3):
        pl.semaphore_signal(barrier, inc=1, device_id={"narrow": (x + k) % 4 * 2 + core}, device_id_type=MESH)
    pl.semaphore_signal(barrier, inc=1, device_id={"narrow": x * 2 + 1 - core}, device_id_type=MESH)

    tile = lax.broadcasted_iota(jnp.int32, (64, 512), 1)
    block = lax.broadcasted_iota(jnp.int32, (64, 512), 0)
    picked = jnp.where(tile // 8 == block, amask_ref[...].astype(jnp.float32), 0.0).astype(jnp.bfloat16)
    tile = lax.broadcasted_iota(jnp.int32, (512, 512), 0)
    row = lax.broadcasted_iota(jnp.int32, (512, 512), 1)
    spread = jnp.where(tile % 8 == row // TILE, 1.0, 0.0).astype(jnp.bfloat16)
    arow[...] = jnp.dot(picked, spread, preferred_element_type=jnp.float32)

    load_amp.wait()

    def mask_block(b, _):
        keep = arow[pl.ds(b, 1), :]
        masked[b] = (amp[b].astype(jnp.float32) * keep).astype(jnp.bfloat16)
        return 0

    lax.fori_loop(0, 64, mask_block, 0, unroll=4)
    pl.semaphore_wait(barrier, 67)

    keep_self = pltpu.make_async_copy(masked.at[me], own.at[me], self_sem.at[0])
    keep_self.start()
    for r in ROW_ORDER:
        to_y = (y + 8 - r) % 8

        def send(i, _, to_y=to_y):
            to = to_y * 8 + (z + i) % 8
            pltpu.make_async_remote_copy(
                src_ref=masked.at[to], dst_ref=own.at[me], send_sem=a2a_send.at[0], recv_sem=a2a_recv.at[y],
                device_id={"wide": to}, device_id_type=MESH,
            ).start()
            return 0

        lax.fori_loop(1 if r == 0 else 0, 8, send, 0)

    col = lax.broadcasted_iota(jnp.int32, (24, 1536), 1)
    tile = lax.broadcasted_iota(jnp.int32, (24, 1536), 0)
    spread = jnp.where(col // TILE == tile, 1.0, 0.0).astype(jnp.bfloat16)
    flags = jnp.dot(imask_ref[...].astype(jnp.bfloat16), spread, preferred_element_type=jnp.float32)
    where = lax.broadcasted_iota(jnp.int32, (8, 1536), 1) // 512 + me
    flags = jnp.where((where >= 1) & (where <= 64), flags, 0.0).astype(jnp.bfloat16)
    load_int.wait()
    for m in range(8):
        rows = pl.ds(m * 64, 64)
        weights[rows, :] = weights[rows, :] * flags[m:m + 1, :]

    def column(r):
        return (y + r) % 8

    def forward(i, r):
        c = column(r)
        span = pl.ds(c * 8, 8)
        count = 7 if r == 0 else 8
        pltpu.make_async_remote_copy(
            src_ref=own.at[pl.ds(0, count)], dst_ref=own.at[pl.ds(0, count)], send_sem=a2a_send.at[0],
            recv_sem=a2a_recv.at[c], device_id={"wide": up}, device_id_type=MESH,
        ).wait_recv()
        if r == 0:
            keep_self.wait()
        for side, (dest, to) in enumerate(((low, up), (high, down))):
            pltpu.make_async_remote_copy(
                src_ref=own.at[span], dst_ref=dest.at[span], send_sem=halo_send.at[side],
                recv_sem=halo_recv.at[side, c], device_id={"wide": to}, device_id_type=MESH,
            ).start()

    def multiply(i, r):
        c = column(r)
        span = pl.ds(c * 8, 8)
        acc = lax.dot_general(
            own[span].reshape(64, 512), weights[:, 512:1024], NT, preferred_element_type=jnp.float32
        )
        for side, (buf, s) in enumerate(((low, 0), (high, 2))):
            pltpu.make_async_remote_copy(
                src_ref=buf.at[span], dst_ref=buf.at[span], send_sem=halo_send.at[side],
                recv_sem=halo_recv.at[side, c], device_id={"wide": up}, device_id_type=MESH,
            ).wait_recv()
            acc += lax.dot_general(
                buf[span].reshape(64, 512), weights[:, s * 512:(s + 1) * 512], NT,
                preferred_element_type=jnp.float32,
            )
        for k in range(4):
            part[i, k] = acc[:, k * 128:(k + 1) * 128]
        for k in (2, 1, 3):
            to = (x + k) % 4
            pltpu.make_async_remote_copy(
                src_ref=part.at[i, to], dst_ref=from_x.at[i, k - 1], send_sem=x_send.at[0],
                recv_sem=x_recv.at[i], device_id={"narrow": to * 2 + core}, device_id_type=MESH,
            ).start()

    def gather(i, r):
        pltpu.make_async_remote_copy(
            src_ref=from_x.at[i], dst_ref=from_x.at[i], send_sem=x_send.at[0],
            recv_sem=x_recv.at[i], device_id={"wide": up}, device_id_type=MESH,
        ).wait_recv()
        mine[i] = part[i, x] + from_x[i, 0] + from_x[i, 1] + from_x[i, 2]
        pltpu.make_async_remote_copy(
            src_ref=mine.at[i], dst_ref=from_core.at[i], send_sem=core_send.at[0],
            recv_sem=core_recv.at[i], device_id={"narrow": x * 2 + 1 - core}, device_id_type=MESH,
        ).start()

    def finish(i, r):
        pltpu.make_async_remote_copy(
            src_ref=mine.at[i], dst_ref=from_core.at[i], send_sem=core_send.at[0],
            recv_sem=core_recv.at[i], device_id={"wide": up}, device_id_type=MESH,
        ).wait_recv()
        total[pl.ds(column(r) * 64, 64), :] = mine[i] + from_core[i]

    lags = ((forward, 0), (multiply, 2), (gather, 4), (finish, 5))
    for step in range(8 + lags[-1][1]):
        for stage, lag in lags:
            i = step - lag
            if 0 <= i < 8:
                stage(i, ROW_ORDER[i])

    turned = total[...].T
    out_ref[...] = jnp.where(core == 0, turned[:64], turned[64:])

    def drain(ref, sem):
        pltpu.make_async_remote_copy(
            src_ref=ref, dst_ref=ref, send_sem=sem, recv_sem=core_recv.at[0],
            device_id={"wide": up}, device_id_type=MESH,
        ).wait_send()

    drain(own.at[pl.ds(0, 63)], a2a_send.at[0])
    drain(own, halo_send.at[0])
    drain(own, halo_send.at[1])
    drain(from_x, x_send.at[0])
    drain(mine, core_send.at[0])


def body(amplitudes, integrals, amplitude_mask, integral_mask):
    bf16, f32 = jnp.bfloat16, jnp.float32
    dma = pltpu.SemaphoreType.DMA
    block = (64, 8, 512)
    return pl.pallas_call(
        kernel,
        out_shape=jax.ShapeDtypeStruct((64, 512), f32),
        in_specs=[
            pl.BlockSpec(memory_space=pl.ANY),
            pl.BlockSpec(memory_space=pl.ANY),
            pl.BlockSpec(memory_space=pltpu.VMEM),
            pl.BlockSpec(memory_space=pltpu.VMEM),
        ],
        out_specs=pl.BlockSpec(memory_space=pltpu.VMEM),
        scratch_shapes=[
            pltpu.VMEM(block, bf16),
            pltpu.VMEM((512, 1536), bf16),
            pltpu.VMEM((64, 512), f32),
            pltpu.VMEM(block, bf16),
            pltpu.VMEM(block, bf16),
            pltpu.VMEM(block, bf16),
            pltpu.VMEM(block, bf16),
            pltpu.VMEM((8, 4, 64, 128), f32),
            pltpu.VMEM((8, 3, 64, 128), f32),
            pltpu.VMEM((8, 64, 128), f32),
            pltpu.VMEM((8, 64, 128), f32),
            pltpu.VMEM((512, 128), f32),
            dma((2,)),
            dma((1,)),
            dma((1,)),
            dma((8,)),
            dma((2,)),
            dma((2, 8)),
            dma((1,)),
            dma((8,)),
            dma((1,)),
            dma((8,)),
        ],
        compiler_params=pltpu.CompilerParams(
            collective_id=0, has_side_effects=True, vmem_limit_bytes=32 * 1024 * 1024
        ),
        name="ladder",
    )(
        amplitudes.reshape(64, 512, 8).transpose(0, 2, 1),
        integrals[0, 0],
        amplitude_mask.T,
        integral_mask[0, 0],
    )


def solution(mesh):
    return jax.shard_map(
        body,
        mesh=mesh,
        in_specs=(
            P("narrow", "wide"),
            P("narrow", "wide", None, None),
            P("narrow", "wide"),
            P("narrow", "wide", None, None),
        ),
        out_specs=P(("narrow", "wide"), None),
        check_vma=False,
    )
```

time: 107 us -> 80.2 us (0.75)
  the two profiles are of different devices: /device:TPU:8 before, /device:TPU:1 now
where the time goes in v1:
time: 80.2 us; the launch traced here: 79.9 us
  Pallas kernels  75.4 us (94%)
  local copies, waits for them, and re-layouts  4.47 us (6%)
    pallas_call x1, Pallas kernels, body(): pl.pallas_call(kernel, out_shape=jax.ShapeDtypeStruct((64, 512), f32), in...  75.4 us
    unnamed x9, local copies, waits for them, and re-layouts  4.47 us

profile of v1, /device:TPU:1, one launch (start us, length us, event | category | flops | bytes accessed | tf_op | source)
XLA Modules:
  0.0 79.9 jit_solution(17807378722958158911)
XLA Ops:
  0.0 0.0 copy-start
  0.0 1.4 %copy-done = bf16[1,1,512,1536]{3,2,1,0:T(8,128)(2,1)S(1)} copy-done((bf16[1,1,512,1536]{3,2,1,0:T(8,128)(2,1)S(1)}, bf16[1,1,512,1536]{3,2,1,0:T(8,128)(2,1)}, u32[]{:S(2)}) %copy-start) | copy-done | bytes 1572888
  1.4 0.0 copy-start.1
  1.4 1.0 %copy-done.1 = bf16[32768,8]{0,1:T(8,128)(2,1)S(1)} copy-done((bf16[32768,8]{0,1:T(8,128)(2,1)S(1)}, bf16[32768,8]{0,1:T(8,128)(2,1)}, u32[]{:S(2)}) %copy-start.1) | copy-done | bytes 524312
  2.5 0.0 copy-start.2
  2.5 0.7 copy-done.2
  3.1 0.0 copy-start.3
  3.1 0.7 copy-done.3
  3.8 75.4 %ladder.1 = f32[64,512]{1,0:T(8,128)S(1)} custom-call(bf16[64,8,512]{2,1,0:T(8,128)(2,1)S(1)} %bitcast.7, bf16[512,1536]{1,0:T(8,128)(2,1)S(1)} %bitcast.6, s32[1,512]{1,0:T(1,128)S(1)} %bitcast.9, s32[8,24]{1,0:T(8,128)S(1)} %bitcast.8), custom_call_target="tpu_custom_call" | custom-call | tf_op jit(solution)/shard_map/ladder/pallas_call | solution.py:173
  79.3 0.7 copy.6
Async XLA Ops:
  0.0 1.4 %copy-start = (bf16[1,1,512,1536]{3,2,1,0:T(8,128)(2,1)S(1)}, bf16[1,1,512,1536]{3,2,1,0:T(8,128)(2,1)}, u32[]{:S(2)}) copy-start(bf16[1,1,512,1536]{3,2,1,0:T(8,128)(2,1)} %param.5) | copy-start | bytes 4718596
  1.4 1.0 %copy-start.1 = (bf16[32768,8]{0,1:T(8,128)(2,1)S(1)}, bf16[32768,8]{0,1:T(8,128)(2,1)}, u32[]{:S(2)}) copy-start(bf16[32768,8]{0,1:T(8,128)(2,1)} %param.4) | copy-start | bytes 1572868
  2.5 0.7 copy-start.2
  3.1 0.7 copy-start.3

commit v2 on v0

v2 whole, which is shorter than its diff:
```python
import jax
import jax.numpy as jnp
from jax import lax
from jax.experimental import pallas as pl
from jax.experimental.pallas import tpu as pltpu
from jax.sharding import PartitionSpec as P

MESH = pl.DeviceIdType.MESH
TILE = 64
NT = (((1,), (1,)), ((), ()))
OFFSETS = (0, 1, 7, 2, 6, 3, 5, 4)
FRONT, HERE, BACK, PASS = range(4)
FRONT_DIRECT, FRONT_CHAIN, BACK_DIRECT, BACK_CHAIN, HERE_SELF, HERE_FORTH, HERE_REAR, PASS_FRONT, PASS_BACK = range(9)
LAGS = (0, 2, 4, 7, 8, 10)


def kernel(
    amp_hbm, int_hbm, amask_ref, imask_ref, out_ref,
    amp, raw, weights, arow, masked, column, near, mine, other, from_core, part, from_x, total,
    load_sem, y_send, y_recv, z_send, pass_sem, z_recv, core_send, core_recv, x_send, x_recv,
):
    me = lax.axis_index("wide")
    nar = lax.axis_index("narrow")
    y, z = me // 8, me % 8
    x, core = nar // 2, nar % 2
    turn = 1 - 2 * core
    has_front = (z + turn >= 0) & (z + turn < 8)
    has_back = (z - turn >= 0) & (z - turn < 8)
    front_w, back_w = me + turn, me - turn
    any_front = (front_w >= 0) & (front_w < 64)
    any_back = (back_w >= 0) & (back_w < 64)
    cross_front = any_front & jnp.logical_not(has_front)
    cross_back = any_back & jnp.logical_not(has_back)
    ring_front, ring_back = y * 8 + (z + 8 + turn) % 8, y * 8 + (z + 8 - turn) % 8
    past_y, prior_y = y + turn, y - turn
    pass_past = jnp.logical_not(has_back) & (past_y >= 0) & (past_y < 8)
    pass_prior = jnp.logical_not(has_front) & (prior_y >= 0) & (prior_y < 8)
    partner = {"narrow": x * 2 + 1 - core}

    def greet(device):
        pl.semaphore_signal(pltpu.get_barrier_semaphore(), inc=1, device_id=device, device_id_type=MESH)

    load_amp = pltpu.make_async_copy(amp_hbm, amp, load_sem.at[0])
    load_int = pltpu.make_async_copy(int_hbm, raw, load_sem.at[1])
    load_amp.start()
    load_int.start()
    for k in (4, 3, 5, 2, 6, 1, 7):
        greet({"wide": (y + k) % 8 * 8 + z})
        greet({"wide": y * 8 + (z + k) % 8})
    for k in (2, 1, 3):
        greet({"narrow": (x + k) % 4 * 2 + core})
    greet(partner)
    pl.when(cross_front)(lambda: greet({"wide": front_w}))
    pl.when(cross_back)(lambda: greet({"wide": back_w}))

    tile = lax.broadcasted_iota(jnp.int32, (64, 512), 1)
    block = lax.broadcasted_iota(jnp.int32, (64, 512), 0)
    picked = jnp.where(tile // 8 == block, amask_ref[...].astype(jnp.float32), 0.0).astype(jnp.bfloat16)
    tile = lax.broadcasted_iota(jnp.int32, (512, 512), 0)
    row = lax.broadcasted_iota(jnp.int32, (512, 512), 1)
    spread = jnp.where(tile % 8 == row // TILE, 1.0, 0.0).astype(jnp.bfloat16)
    arow[...] = jnp.dot(picked, spread, preferred_element_type=jnp.float32)
    load_amp.wait()

    def mask_block(b, _):
        keep = arow[pl.ds(b, 1), :]
        masked[b] = (amp[b].astype(jnp.float32) * keep).astype(jnp.bfloat16)
        return 0

    lax.fori_loop(0, 64, mask_block, 0, unroll=4)

    @pl.when(jnp.logical_not(any_front))
    def _():
        near[FRONT] = jnp.zeros((8, 8, 8, 512), jnp.bfloat16)

    @pl.when(jnp.logical_not(any_back))
    def _():
        near[BACK] = jnp.zeros((8, 8, 8, 512), jnp.bfloat16)

    pl.semaphore_wait(pltpu.get_barrier_semaphore(), 18 + cross_front.astype(jnp.int32) + cross_back.astype(jnp.int32))

    for offset in OFFSETS[1:]:
        to_y = (y + 8 - offset) % 8
        pltpu.make_async_remote_copy(
            src_ref=masked.at[pl.ds(to_y * 8, 8)], dst_ref=column.at[y], send_sem=y_send.at[0],
            recv_sem=y_recv.at[y], device_id={"wide": to_y * 8 + z}, device_id_type=MESH,
        ).start()

    def source(i):
        return (y + OFFSETS[i]) % 8

    def spread_row(i):
        c = source(i)
        if i > 0:
            pltpu.make_async_copy(column.at[0], column.at[0], y_recv.at[c]).wait()
        for rel in (0, 1, 7, 2, 6, 3, 5, 4):
            to_z = (z + 8 + turn * rel) % 8
            slab = masked.at[y * 8 + to_z] if i == 0 else column.at[c, to_z]
            if rel == 0:
                to, buf, spot, group = to_z, HERE, 0, HERE_SELF
            elif rel <= 4:
                ahead = to_z - turn
                inside = (ahead >= 0) & (ahead < 8)
                to, spot = (ahead + 8) % 8, rel - 1
                buf, group = jnp.where(inside, FRONT, PASS), jnp.where(inside, FRONT_DIRECT, PASS_FRONT)
            else:
                ahead = to_z + turn
                inside = (ahead >= 0) & (ahead < 8)
                to, spot = (ahead + 8) % 8, (rel + 1) % 8
                buf, group = jnp.where(inside, BACK, PASS), jnp.where(inside, BACK_DIRECT, PASS_BACK)
            if rel in (0, 1, 7):
                pltpu.make_async_copy(slab, near.at[buf, c, spot], z_recv.at[group, c]).start()
            else:
                pltpu.make_async_remote_copy(
                    src_ref=slab, dst_ref=near.at[buf, c, spot], send_sem=z_send.at[0],
                    recv_sem=z_recv.at[group, c], device_id={"wide": y * 8 + to}, device_id_type=MESH,
                ).start()

    def arrive(group, c, count):
        span = near.at[HERE, c, pl.ds(0, count)]
        pltpu.make_async_copy(span, span, z_recv.at[group, c]).wait()

    def hand(way, buf, c, first, count, to, to_buf, to_first, group):
        pltpu.make_async_remote_copy(
            src_ref=near.at[buf, c, pl.ds(first, count)], dst_ref=near.at[to_buf, c, pl.ds(to_first, count)],
            send_sem=pass_sem.at[way], recv_sem=z_recv.at[group, c], device_id={"wide": to}, device_id_type=MESH,
        ).start()

    def enter(i):
        c = source(i)
        arrive(jnp.where(has_front, FRONT_DIRECT, PASS_FRONT), c, 4)
        buf = jnp.where(has_front, FRONT, PASS)
        hand(0, buf, c, 0, 4, ring_front, HERE, 1, HERE_FORTH)

        @pl.when(pass_prior)
        def _():
            hand(2, PASS, c, 0, 4, prior_y * 8 + z, FRONT, 0, FRONT_DIRECT)

        arrive(jnp.where(has_back, BACK_DIRECT, PASS_BACK), c, 3)
        buf = jnp.where(has_back, BACK, PASS)
        hand(1, buf, c, 6, 2, ring_back, HERE, 5, HERE_REAR)
        hand(1, buf, c, 0, 1, ring_back, HERE, 7, HERE_REAR)

        @pl.when(pass_past)
        def _():
            hand(2, PASS, c, 6, 2, past_y * 8 + z, BACK, 6, BACK_DIRECT)
            hand(2, PASS, c, 0, 1, past_y * 8 + z, BACK, 0, BACK_DIRECT)

    def relay(i):
        c = source(i)
        arrive(HERE_SELF, c, 1)
        arrive(HERE_FORTH, c, 4)

        @pl.when(any_front)
        def _():
            hand(0, HERE, c, 0, 5, front_w, BACK, 1, BACK_CHAIN)

        arrive(HERE_REAR, c, 3)

        @pl.when(any_back)
        def _():
            hand(1, HERE, c, 5, 3, back_w, FRONT, 4, FRONT_CHAIN)
            hand(1, HERE, c, 0, 1, back_w, FRONT, 7, FRONT_CHAIN)

    def multiply(i):
        c = source(i)

        @pl.when(any_front)
        def _():
            arrive(FRONT_CHAIN, c, 4)

        @pl.when(cross_front)
        def _():
            arrive(FRONT_DIRECT, c, 4)

        @pl.when(any_back)
        def _():
            arrive(BACK_CHAIN, c, 5)

        @pl.when(cross_back)
        def _():
            arrive(BACK_DIRECT, c, 3)

        acc = None
        for buf in (HERE, FRONT, BACK):
            start = pl.multiple_of((1 + turn * (1 - buf)) * 512, 512)
            term = lax.dot_general(
                near[buf, c].reshape(64, 512), weights[:, pl.ds(start, 512)], NT, preferred_element_type=jnp.float32
            )
            acc = term if acc is None else acc + term
        mine[i] = acc[:, :256]
        other[i] = acc[:, 256:]
        pltpu.make_async_remote_copy(
            src_ref=other.at[i], dst_ref=from_core.at[i], send_sem=core_send.at[0],
            recv_sem=core_recv.at[i], device_id=partner, device_id_type=MESH,
        ).start()

    low_lanes = lax.broadcasted_iota(jnp.int32, (32, 128), 1) < 64

    def swap(i):
        pltpu.make_async_copy(from_core.at[i], from_core.at[i], core_recv.at[i]).wait()
        for pair in range(2):
            lanes = slice(pair * 128, pair * 128 + 128)
            rows = [
                mine[i, p * 8:p * 8 + 8, lanes] + from_core[i, (8 - p) % 8 * 8:(8 - p) % 8 * 8 + 8, lanes]
                for p in range(8)
            ]
            upper, lower = jnp.concatenate(rows[:4], 0), jnp.concatenate(rows[4:], 0)
            part[i, 2 * pair] = jnp.where(low_lanes, upper, pltpu.roll(lower, 64, 1))
            part[i, 2 * pair + 1] = jnp.where(low_lanes, pltpu.roll(upper, 64, 1), lower)
        for k in (2, 1, 3):
            to = (x + k) % 4
            pltpu.make_async_remote_copy(
                src_ref=part.at[i, to], dst_ref=from_x.at[i, k - 1], send_sem=x_send.at[0],
                recv_sem=x_recv.at[i], device_id={"narrow": to * 2 + core}, device_id_type=MESH,
            ).start()

    def finish(i):
        c = source(i)
        pltpu.make_async_copy(from_x.at[i], from_x.at[i], x_recv.at[i]).wait()
        done = part[i, x] + from_x[i, 0] + from_x[i, 1] + from_x[i, 2]
        turned = pltpu.roll(done, 64, 1)
        for p in range(8):
            at = (z + 8 - turn * p) % 8
            total[c * 8 + at] = (done if p < 4 else turned)[p % 4 * 8:p % 4 * 8 + 8]

    def mask_weights():
        col = lax.broadcasted_iota(jnp.int32, (24, 1536), 1)
        tile = lax.broadcasted_iota(jnp.int32, (24, 1536), 0)
        spread = jnp.where(col // TILE == tile, 1.0, 0.0).astype(jnp.bfloat16)
        flags = jnp.dot(imask_ref[...].astype(jnp.bfloat16), spread, preferred_element_type=jnp.float32)
        where = lax.broadcasted_iota(jnp.int32, (8, 1536), 1) // 512 + me
        flags = jnp.where((where >= 1) & (where <= 64), flags, 0.0).astype(jnp.bfloat16)
        load_int.wait()
        for m in range(8):
            to = pl.multiple_of(((m % 2 + core) % 2 * 4 + m // 2) * 64, 64)
            weights[pl.ds(to, 64), :] = raw[m * 64:m * 64 + 64, :] * flags[m:m + 1, :]

    stages = (spread_row, enter, relay, multiply, swap, finish)
    for step in range(8 + LAGS[-1]):
        for stage, lag in zip(stages, LAGS):
            if 0 <= step - lag < 8:
                stage(step - lag)
            if step == 0 and stage is spread_row:
                mask_weights()

    out_ref[...] = total[...].reshape(512, 128).T[:64]

    def drain(ref, sem):
        pltpu.make_async_copy(ref, ref, sem).wait()

    drain(near.at[0, pl.ds(0, 7)], y_send.at[0])
    drain(near.at[0, pl.ds(0, 5)], z_send.at[0])
    drain(near.at[0, pl.ds(0, 4)], pass_sem.at[0])
    drain(near.at[0, pl.ds(0, 3)], pass_sem.at[1])

    @pl.when(any_front)
    def _():
        drain(near.at[0, pl.ds(0, 5)], pass_sem.at[0])

    @pl.when(any_back)
    def _():
        drain(near.at[0, pl.ds(0, 4)], pass_sem.at[1])

    @pl.when(pass_prior)
    def _():
        drain(near.at[0, pl.ds(0, 4)], pass_sem.at[2])

    @pl.when(pass_past)
    def _():
        drain(near.at[0, pl.ds(0, 3)], pass_sem.at[2])

    drain(other, core_send.at[0])
    drain(from_x, x_send.at[0])


def body(amplitudes, integrals, amplitude_mask, integral_mask):
    bf16, f32 = jnp.bfloat16, jnp.float32
    dma = pltpu.SemaphoreType.DMA
    return pl.pallas_call(
        kernel,
        out_shape=jax.ShapeDtypeStruct((64, 512), f32),
        in_specs=[
            pl.BlockSpec(memory_space=pl.ANY),
            pl.BlockSpec(memory_space=pl.ANY),
            pl.BlockSpec(memory_space=pltpu.VMEM),
            pl.BlockSpec(memory_space=pltpu.VMEM),
        ],
        out_specs=pl.BlockSpec(memory_space=pltpu.VMEM),
        scratch_shapes=[
            pltpu.VMEM((64, 8, 512), bf16),
            pltpu.VMEM((512, 1536), bf16),
            pltpu.VMEM((512, 1536), bf16),
            pltpu.VMEM((64, 512), f32),
            pltpu.VMEM((64, 8, 512), bf16),
            pltpu.VMEM((8, 8, 8, 512), bf16),
            pltpu.VMEM((4, 8, 8, 8, 512), bf16),
            pltpu.VMEM((8, 64, 256), f32),
            pltpu.VMEM((8, 64, 256), f32),
            pltpu.VMEM((8, 64, 256), f32),
            pltpu.VMEM((8, 4, 32, 128), f32),
            pltpu.VMEM((8, 3, 32, 128), f32),
            pltpu.VMEM((64, 8, 128), f32),
            dma((2,)),
            dma((1,)),
            dma((8,)),
            dma((1,)),
            dma((3,)),
            dma((9, 8)),
            dma((1,)),
            dma((8,)),
            dma((1,)),
            dma((8,)),
        ],
        compiler_params=pltpu.CompilerParams(
            collective_id=0, has_side_effects=True, vmem_limit_bytes=60 * 1024 * 1024
        ),
        name="ladder",
    )(
        amplitudes.reshape(64, 512, 8).transpose(0, 2, 1),
        integrals[0, 0],
        amplitude_mask.T,
        integral_mask[0, 0],
    )


def solution(mesh):
    return jax.shard_map(
        body,
        mesh=mesh,
        in_specs=(
            P("narrow", "wide"),
            P("narrow", "wide", None, None),
            P("narrow", "wide"),
            P("narrow", "wide", None, None),
        ),
        out_specs=P(("narrow", "wide"), None),
        check_vma=False,
    )
```

time: 107 us -> 56.5 us (0.53)
  Pallas kernels: 0 us -> 54.7 us
  waiting for transfers between devices: 46.2 us -> 0 us
  blocking collectives: 35 us -> 0 us
  between operations: 13.5 us -> 0.01 us
  starting transfers between devices: 5.84 us -> 0 us
  matrix products: 3.36 us -> 0 us
  other arithmetic: 2.05 us -> 0 us
    pallas_call x0 -> x1, Pallas kernels: none -> 54.7 us  [body(): pl.pallas_call(kernel, out_shape=jax.ShapeDtypeStruct((64, 512), f32), in...]
    all_to_all x1 -> x0, blocking collectives: 35 us -> none  [body(): lax.all_to_all(masked, 'wide', split_axis=0, concat_axis=1, tiled=True)]
    reduce_scatter x1 -> x0, waiting for transfers between devices: 34.3 us -> none  [body(): lax.psum_scatter(jnp.dot(weights, nearby, preferred_element_type=jnp.floa...]
    ppermute x2 -> x0, waiting for transfers between devices: 11.9 us -> none  [the longest x1 6.42 us: with_halo(): lax.ppermute(head, axis, [((i + 1) % count, i) for i in range(ends)])]
    ppermute x2 -> x0, starting transfers between devices: 5.83 us -> none  [the longest x1 3.28 us: with_halo(): lax.ppermute(head, axis, [((i + 1) % count, i) for i in range(ends)])]
    dot_general x1 -> x0, matrix products: 3.36 us -> none  [body(): jnp.dot(weights, nearby, preferred_element_type=jnp.float32)]
    mul x2 -> x0, other arithmetic: 1.23 us -> none  [the longest x1 1.12 us: body(): masked = amplitudes * tile_mask]
  transfers between devices with their start and end apart: 3 -> 0, of which waited for: 3 -> 0; matrix products, arithmetic and copies ran while one was open for 1% -> 0% of each run, Pallas kernels for 0% -> 0%
where the time goes in v2:
time: 56.5 us; the launch traced here: 56.3 us
  Pallas kernels  54.7 us (97%)
  local copies, waits for them, and re-layouts  1.57 us (3%)
    pallas_call x1, Pallas kernels, body(): pl.pallas_call(kernel, out_shape=jax.ShapeDtypeStruct((64, 512), f32), in...  54.7 us
    unnamed x1, local copies, waits for them, and re-layouts  1.57 us

profile of v2, /device:TPU:8, one launch (start us, length us, event | category | flops | bytes accessed | tf_op | source)
XLA Modules:
  0.0 56.3 jit_solution(11006330419963736007)
XLA Ops:
  0.0 54.7 %ladder.1 = f32[64,512]{1,0:T(8,128)} custom-call(bf16[64,8,512]{2,1,0:T(8,128)(2,1)} %bitcast.7, bf16[512,1536]{1,0:T(8,128)(2,1)} %bitcast.6, s32[1,512]{1,0:T(1,128)} %bitcast.9, s32[8,24]{1,0:T(8,128)} %bitcast.8), custom_call_target="tpu_custom_call" | custom-call | tf_op jit(solution)/shard_map/ladder/pallas_call | solution.py:280
  54.7 1.6 %copy.6 = f32[64,512]{1,0:T(8,128)} copy(f32[64,512]{1,0:T(8,128)} %ladder.1) | data formatting | bytes 262144

commit v3 on v2

--- a/solution.py
+++ b/solution.py
@@ -8,16 +8,18 @@
 MESH = pl.DeviceIdType.MESH
 TILE = 64
 NT = (((1,), (1,)), ((), ()))
-OFFSETS = (0, 1, 7, 2, 6, 3, 5, 4)
+OFFSETS = (0, 7, 1, 6, 2, 5, 3, 4)
+TURNS = ((0, 1, 2, 3, 4, 5, 6, 7), (1, 0, 3, 2, 5, 4, 7, 6), (0, 2, 1, 4, 3, 6, 5, 7))
 FRONT, HERE, BACK, PASS = range(4)
 FRONT_DIRECT, FRONT_CHAIN, BACK_DIRECT, BACK_CHAIN, HERE_SELF, HERE_FORTH, HERE_REAR, PASS_FRONT, PASS_BACK = range(9)
-LAGS = (0, 2, 4, 7, 8, 10)
+LEAD = 4
+LAGS = (0, 2, 5, 7, 10)
 
 
 def kernel(
     amp_hbm, int_hbm, amask_ref, imask_ref, out_ref,
-    amp, raw, weights, arow, masked, column, near, mine, other, from_core, part, from_x, total,
-    load_sem, y_send, y_recv, z_send, pass_sem, z_recv, core_send, core_recv, x_send, x_recv,
+    amp, raw, weights, keep, masked, near, mine, other, from_core, part, from_x, total,
+    amp_sem, load_sem, z_send, pass_sem, z_recv, core_send, core_recv, x_send, x_recv,
 ):
     me = lax.axis_index("wide")
     nar = lax.axis_index("narrow")
@@ -40,34 +42,20 @@
     def greet(device):
         pl.semaphore_signal(pltpu.get_barrier_semaphore(), inc=1, device_id=device, device_id_type=MESH)
 
-    load_amp = pltpu.make_async_copy(amp_hbm, amp, load_sem.at[0])
-    load_int = pltpu.make_async_copy(int_hbm, raw, load_sem.at[1])
-    load_amp.start()
-    load_int.start()
-    for k in (4, 3, 5, 2, 6, 1, 7):
-        greet({"wide": (y + k) % 8 * 8 + z})
-        greet({"wide": y * 8 + (z + k) % 8})
+    def greet_wide(i, _):
+        greet({"wide": (me + i) % 64})
+        return 0
+
+    lax.fori_loop(32, 64, greet_wide, 0)
+    lax.fori_loop(1, 32, greet_wide, 0)
     for k in (2, 1, 3):
         greet({"narrow": (x + k) % 4 * 2 + core})
     greet(partner)
-    pl.when(cross_front)(lambda: greet({"wide": front_w}))
-    pl.when(cross_back)(lambda: greet({"wide": back_w}))
-
-    tile = lax.broadcasted_iota(jnp.int32, (64, 512), 1)
-    block = lax.broadcasted_iota(jnp.int32, (64, 512), 0)
-    picked = jnp.where(tile // 8 == block, amask_ref[...].astype(jnp.float32), 0.0).astype(jnp.bfloat16)
-    tile = lax.broadcasted_iota(jnp.int32, (512, 512), 0)
-    row = lax.broadcasted_iota(jnp.int32, (512, 512), 1)
-    spread = jnp.where(tile % 8 == row // TILE, 1.0, 0.0).astype(jnp.bfloat16)
-    arow[...] = jnp.dot(picked, spread, preferred_element_type=jnp.float32)
-    load_amp.wait()
-
-    def mask_block(b, _):
-        keep = arow[pl.ds(b, 1), :]
-        masked[b] = (amp[b].astype(jnp.float32) * keep).astype(jnp.bfloat16)
-        return 0
-
-    lax.fori_loop(0, 64, mask_block, 0, unroll=4)
+    for i in range(8):
+        blocks = pl.ds((y + 8 - OFFSETS[i]) % 8 * 8, 8)
+        pltpu.make_async_copy(amp_hbm.at[blocks], amp.at[blocks], amp_sem.at[i]).start()
+    load_int = pltpu.make_async_copy(int_hbm, raw, load_sem.at[0])
+    load_int.start()
 
     @pl.when(jnp.logical_not(any_front))
     def _():
@@ -77,25 +65,29 @@
     def _():
         near[BACK] = jnp.zeros((8, 8, 8, 512), jnp.bfloat16)
 
-    pl.semaphore_wait(pltpu.get_barrier_semaphore(), 18 + cross_front.astype(jnp.int32) + cross_back.astype(jnp.int32))
-
-    for offset in OFFSETS[1:]:
-        to_y = (y + 8 - offset) % 8
-        pltpu.make_async_remote_copy(
-            src_ref=masked.at[pl.ds(to_y * 8, 8)], dst_ref=column.at[y], send_sem=y_send.at[0],
-            recv_sem=y_recv.at[y], device_id={"wide": to_y * 8 + z}, device_id_type=MESH,
-        ).start()
+    tile = lax.broadcasted_iota(jnp.int32, (512, 512), 1)
+    row = lax.broadcasted_iota(jnp.int32, (512, 512), 0)
+    picked = jnp.where(tile // 8 == row // 8, amask_ref[...].astype(jnp.float32), 0.0).astype(jnp.bfloat16)
+    spread = jnp.where(row % 8 == tile // TILE, 1.0, 0.0).astype(jnp.bfloat16)
+    keep[...] = jnp.dot(picked, spread, preferred_element_type=jnp.float32).astype(jnp.bfloat16).reshape(64, 8, 512)
+
+    def mask_row(i):
+        to_y = (y + 8 - OFFSETS[i]) % 8
+        blocks = pl.ds(to_y * 8, 8)
+        pltpu.make_async_copy(amp_hbm.at[blocks], amp.at[blocks], amp_sem.at[i]).wait()
+        masked[blocks] = amp[blocks] * keep[blocks]
+
+    mask_row(0)
+    mask_row(1)
+    pl.semaphore_wait(pltpu.get_barrier_semaphore(), 67)
 
     def source(i):
         return (y + OFFSETS[i]) % 8
 
-    def spread_row(i):
-        c = source(i)
-        if i > 0:
-            pltpu.make_async_copy(column.at[0], column.at[0], y_recv.at[c]).wait()
+    def send(i):
+        to_y = (y + 8 - OFFSETS[i]) % 8
         for rel in (0, 1, 7, 2, 6, 3, 5, 4):
             to_z = (z + 8 + turn * rel) % 8
-            slab = masked.at[y * 8 + to_z] if i == 0 else column.at[c, to_z]
             if rel == 0:
                 to, buf, spot, group = to_z, HERE, 0, HERE_SELF
             elif rel <= 4:
@@ -108,12 +100,13 @@
                 inside = (ahead >= 0) & (ahead < 8)
                 to, spot = (ahead + 8) % 8, (rel + 1) % 8
                 buf, group = jnp.where(inside, BACK, PASS), jnp.where(inside, BACK_DIRECT, PASS_BACK)
-            if rel in (0, 1, 7):
-                pltpu.make_async_copy(slab, near.at[buf, c, spot], z_recv.at[group, c]).start()
+            slab, place, sem = masked.at[to_y * 8 + to_z], near.at[buf, y, spot], z_recv.at[group, y]
+            if i == 0 and rel in (0, 1, 7):
+                pltpu.make_async_copy(slab, place, sem).start()
             else:
                 pltpu.make_async_remote_copy(
-                    src_ref=slab, dst_ref=near.at[buf, c, spot], send_sem=z_send.at[0],
-                    recv_sem=z_recv.at[group, c], device_id={"wide": y * 8 + to}, device_id_type=MESH,
+                    src_ref=slab, dst_ref=place, send_sem=z_send.at[0], recv_sem=sem,
+                    device_id={"wide": to_y * 8 + to}, device_id_type=MESH,
                 ).start()
 
     def arrive(group, c, count):
@@ -162,8 +155,12 @@
             hand(1, HERE, c, 5, 3, back_w, FRONT, 4, FRONT_CHAIN)
             hand(1, HERE, c, 0, 1, back_w, FRONT, 7, FRONT_CHAIN)
 
+    def turn_of(i):
+        inner, first, last = (OFFSETS[order[i]] for order in TURNS)
+        return (y + jnp.where(z == 0, first, jnp.where(z == 7, last, inner))) % 8
+
     def multiply(i):
-        c = source(i)
+        c = turn_of(i)
 
         @pl.when(any_front)
         def _():
@@ -216,7 +213,7 @@
             ).start()
 
     def finish(i):
-        c = source(i)
+        c = turn_of(i)
         pltpu.make_async_copy(from_x.at[i], from_x.at[i], x_recv.at[i]).wait()
         done = part[i, x] + from_x[i, 0] + from_x[i, 1] + from_x[i, 2]
         turned = pltpu.roll(done, 64, 1)
@@ -236,21 +233,27 @@
             to = pl.multiple_of(((m % 2 + core) % 2 * 4 + m // 2) * 64, 64)
             weights[pl.ds(to, 64), :] = raw[m * 64:m * 64 + 64, :] * flags[m:m + 1, :]
 
-    stages = (spread_row, enter, relay, multiply, swap, finish)
+    for i in range(8):
+        if i > 1:
+            mask_row(i)
+        if i < LEAD:
+            send(i)
+    mask_weights()
+    stages = (enter, relay, multiply, swap, finish)
     for step in range(8 + LAGS[-1]):
+        if step + LEAD < 8:
+            send(step + LEAD)
         for stage, lag in zip(stages, LAGS):
             if 0 <= step - lag < 8:
                 stage(step - lag)
-            if step == 0 and stage is spread_row:
-                mask_weights()
 
     out_ref[...] = total[...].reshape(512, 128).T[:64]
 
     def drain(ref, sem):
         pltpu.make_async_copy(ref, ref, sem).wait()
 
-    drain(near.at[0, pl.ds(0, 7)], y_send.at[0])
-    drain(near.at[0, pl.ds(0, 5)], z_send.at[0])
+    drain(near.at[0, pl.ds(0, 7)], z_send.at[0])
+    drain(near.at[0, 7, pl.ds(0, 5)], z_send.at[0])
     drain(near.at[0, pl.ds(0, 4)], pass_sem.at[0])
     drain(near.at[0, pl.ds(0, 3)], pass_sem.at[1])
 
@@ -291,9 +294,8 @@
             pltpu.VMEM((64, 8, 512), bf16),
             pltpu.VMEM((512, 1536), bf16),
             pltpu.VMEM((512, 1536), bf16),
-            pltpu.VMEM((64, 512), f32),
             pltpu.VMEM((64, 8, 512), bf16),
-            pltpu.VMEM((8, 8, 8, 512), bf16),
+            pltpu.VMEM((64, 8, 512), bf16),
             pltpu.VMEM((4, 8, 8, 8, 512), bf16),
             pltpu.VMEM((8, 64, 256), f32),
             pltpu.VMEM((8, 64, 256), f32),
@@ -301,9 +303,8 @@
             pltpu.VMEM((8, 4, 32, 128), f32),
             pltpu.VMEM((8, 3, 32, 128), f32),
             pltpu.VMEM((64, 8, 128), f32),
-            dma((2,)),
+            dma((8,)),
             dma((1,)),
-            dma((8,)),
             dma((1,)),
             dma((3,)),
             dma((9, 8)),

time: 56.5 us -> 52.5 us (0.929)
  Pallas kernels: 54.7 us -> 50.8 us
    pallas_call x1, Pallas kernels: 54.7 us -> 50.8 us  [body(): pl.pallas_call(kernel, out_shape=jax.ShapeDtypeStruct((64, 512), f32), in...]
where the time goes in v3:
time: 52.5 us; the launch traced here: 52.3 us
  Pallas kernels  50.8 us (97%)
  local copies, waits for them, and re-layouts  1.57 us (3%)
    pallas_call x1, Pallas kernels, body(): pl.pallas_call(kernel, out_shape=jax.ShapeDtypeStruct((64, 512), f32), in...  50.8 us
    unnamed x1, local copies, waits for them, and re-layouts  1.57 us

profile of v3, /device:TPU:8, one launch (start us, length us, event | category | flops | bytes accessed | tf_op | source)
XLA Modules:
  0.0 52.3 jit_solution(15241268491500276400)
XLA Ops:
  0.0 50.8 %ladder.1 = f32[64,512]{1,0:T(8,128)} custom-call(bf16[64,8,512]{2,1,0:T(8,128)(2,1)} %bitcast.7, bf16[512,1536]{1,0:T(8,128)(2,1)} %bitcast.6, s32[1,512]{1,0:T(1,128)} %bitcast.9, s32[8,24]{1,0:T(8,128)} %bitcast.8), custom_call_target="tpu_custom_call" | custom-call | tf_op jit(solution)/shard_map/ladder/pallas_call | solution.py:283
  50.8 1.6 %copy.6 = f32[64,512]{1,0:T(8,128)} copy(f32[64,512]{1,0:T(8,128)} %ladder.1) | data formatting | bytes 262144

commit v4 on v3

--- a/solution.py
+++ b/solution.py
@@ -13,13 +13,13 @@
 FRONT, HERE, BACK, PASS = range(4)
 FRONT_DIRECT, FRONT_CHAIN, BACK_DIRECT, BACK_CHAIN, HERE_SELF, HERE_FORTH, HERE_REAR, PASS_FRONT, PASS_BACK = range(9)
 LEAD = 4
-LAGS = (0, 2, 5, 7, 10)
+LAGS = (0, 2, 5, 6, 9)
 
 
 def kernel(
     amp_hbm, int_hbm, amask_ref, imask_ref, out_ref,
     amp, raw, weights, keep, masked, near, mine, other, from_core, part, from_x, total,
-    amp_sem, load_sem, z_send, pass_sem, z_recv, core_send, core_recv, x_send, x_recv,
+    row_in, amp_sem, load_sem, z_send, pass_sem, z_recv, core_send, core_recv, x_send, x_recv,
 ):
     me = lax.axis_index("wide")
     nar = lax.axis_index("narrow")
@@ -42,12 +42,9 @@
     def greet(device):
         pl.semaphore_signal(pltpu.get_barrier_semaphore(), inc=1, device_id=device, device_id_type=MESH)
 
-    def greet_wide(i, _):
-        greet({"wide": (me + i) % 64})
-        return 0
-
-    lax.fori_loop(32, 64, greet_wide, 0)
-    lax.fori_loop(1, 32, greet_wide, 0)
+    for k in (4, 3, 5, 2, 6, 1, 7):
+        greet({"wide": y * 8 + (z + k) % 8})
+        greet({"wide": (y + k) % 8 * 8 + z})
     for k in (2, 1, 3):
         greet({"narrow": (x + k) % 4 * 2 + core})
     greet(partner)
@@ -79,13 +76,17 @@
 
     mask_row(0)
     mask_row(1)
-    pl.semaphore_wait(pltpu.get_barrier_semaphore(), 67)
+    pl.semaphore_wait(pltpu.get_barrier_semaphore(), 18)
+    for k in (4, 3, 5, 2, 6, 1, 7):
+        pl.semaphore_signal(row_in.at[y], inc=1, device_id={"wide": (y + k) % 8 * 8 + z}, device_id_type=MESH)
 
     def source(i):
         return (y + OFFSETS[i]) % 8
 
     def send(i):
         to_y = (y + 8 - OFFSETS[i]) % 8
+        if i > 0:
+            pl.semaphore_wait(row_in.at[to_y], 1)
         for rel in (0, 1, 7, 2, 6, 3, 5, 4):
             to_z = (z + 8 + turn * rel) % 8
             if rel == 0:
@@ -233,11 +234,11 @@
             to = pl.multiple_of(((m % 2 + core) % 2 * 4 + m // 2) * 64, 64)
             weights[pl.ds(to, 64), :] = raw[m * 64:m * 64 + 64, :] * flags[m:m + 1, :]
 
-    for i in range(8):
-        if i > 1:
-            mask_row(i)
-        if i < LEAD:
-            send(i)
+    send(0)
+    for i in range(2, 8):
+        mask_row(i)
+    for i in range(1, LEAD):
+        send(i)
     mask_weights()
     stages = (enter, relay, multiply, swap, finish)
     for step in range(8 + LAGS[-1]):
@@ -303,6 +304,7 @@
             pltpu.VMEM((8, 4, 32, 128), f32),
             pltpu.VMEM((8, 3, 32, 128), f32),
             pltpu.VMEM((64, 8, 128), f32),
+            pltpu.SemaphoreType.REGULAR((8,)),
             dma((8,)),
             dma((1,)),
             dma((1,)),

time: 52.5 us -> 51.6 us (0.983)
  Pallas kernels: 50.8 us -> 49.8 us
    pallas_call x1, Pallas kernels: 50.8 us -> 49.8 us  [body(): pl.pallas_call(kernel, out_shape=jax.ShapeDtypeStruct((64, 512), f32), in...]
where the time goes in v4:
time: 51.6 us; the launch traced here: 51.4 us
  Pallas kernels  49.8 us (97%)
  local copies, waits for them, and re-layouts  1.57 us (3%)
    pallas_call x1, Pallas kernels, body(): pl.pallas_call(kernel, out_shape=jax.ShapeDtypeStruct((64, 512), f32), in...  49.8 us
    unnamed x1, local copies, waits for them, and re-layouts  1.57 us

profile of v4, /device:TPU:8, one launch (start us, length us, event | category | flops | bytes accessed | tf_op | source)
XLA Modules:
  0.0 51.4 jit_solution(9525041688163400597)
XLA Ops:
  0.0 49.8 %ladder.1 = f32[64,512]{1,0:T(8,128)} custom-call(bf16[64,8,512]{2,1,0:T(8,128)(2,1)} %bitcast.7, bf16[512,1536]{1,0:T(8,128)(2,1)} %bitcast.6, s32[1,512]{1,0:T(1,128)} %bitcast.9, s32[8,24]{1,0:T(8,128)} %bitcast.8), custom_call_target="tpu_custom_call" | custom-call | tf_op jit(solution)/shard_map/ladder/pallas_call | solution.py:284
  49.9 1.6 %copy.6 = f32[64,512]{1,0:T(8,128)} copy(f32[64,512]{1,0:T(8,128)} %ladder.1) | data formatting | bytes 262144

commit v5 on v4

--- a/solution.py
+++ b/solution.py
@@ -7,19 +7,18 @@
 
 MESH = pl.DeviceIdType.MESH
 TILE = 64
-NT = (((1,), (1,)), ((), ()))
 OFFSETS = (0, 7, 1, 6, 2, 5, 3, 4)
 TURNS = ((0, 1, 2, 3, 4, 5, 6, 7), (1, 0, 3, 2, 5, 4, 7, 6), (0, 2, 1, 4, 3, 6, 5, 7))
 FRONT, HERE, BACK, PASS = range(4)
 FRONT_DIRECT, FRONT_CHAIN, BACK_DIRECT, BACK_CHAIN, HERE_SELF, HERE_FORTH, HERE_REAR, PASS_FRONT, PASS_BACK = range(9)
 LEAD = 4
-LAGS = (0, 2, 5, 6, 9)
+LAGS = (0, 2, 5, 6, 10)
 
 
 def kernel(
-    amp_hbm, int_hbm, amask_ref, imask_ref, out_ref,
-    amp, raw, weights, keep, masked, near, mine, other, from_core, part, from_x, total,
-    row_in, amp_sem, load_sem, z_send, pass_sem, z_recv, core_send, core_recv, x_send, x_recv,
+    amp_hbm, int_hbm, amask_hbm, imask_hbm, out_hbm,
+    out, amask, imask, flag_rows, amp, raw, weights, keep, masked, near, mine, other, from_core, part, from_x, total,
+    row_in, mask_sem, amp_sem, load_sem, z_send, pass_sem, z_recv, core_send, core_recv, x_send, x_recv,
 ):
     me = lax.axis_index("wide")
     nar = lax.axis_index("narrow")
@@ -48,11 +47,15 @@
     for k in (2, 1, 3):
         greet({"narrow": (x + k) % 4 * 2 + core})
     greet(partner)
+    load_amask = pltpu.make_async_copy(amask_hbm, amask, mask_sem.at[0])
+    load_imask = pltpu.make_async_copy(imask_hbm, imask, mask_sem.at[1])
+    load_amask.start()
     for i in range(8):
         blocks = pl.ds((y + 8 - OFFSETS[i]) % 8 * 8, 8)
         pltpu.make_async_copy(amp_hbm.at[blocks], amp.at[blocks], amp_sem.at[i]).start()
     load_int = pltpu.make_async_copy(int_hbm, raw, load_sem.at[0])
     load_int.start()
+    load_imask.start()
 
     @pl.when(jnp.logical_not(any_front))
     def _():
@@ -64,7 +67,8 @@
 
     tile = lax.broadcasted_iota(jnp.int32, (512, 512), 1)
     row = lax.broadcasted_iota(jnp.int32, (512, 512), 0)
-    picked = jnp.where(tile // 8 == row // 8, amask_ref[...].astype(jnp.float32), 0.0).astype(jnp.bfloat16)
+    load_amask.wait()
+    picked = jnp.where(tile // 8 == row // 8, amask[...].astype(jnp.float32), 0.0).astype(jnp.bfloat16)
     spread = jnp.where(row % 8 == tile // TILE, 1.0, 0.0).astype(jnp.bfloat16)
     keep[...] = jnp.dot(picked, spread, preferred_element_type=jnp.float32).astype(jnp.bfloat16).reshape(64, 8, 512)
 
@@ -182,8 +186,8 @@
         acc = None
         for buf in (HERE, FRONT, BACK):
             start = pl.multiple_of((1 + turn * (1 - buf)) * 512, 512)
-            term = lax.dot_general(
-                near[buf, c].reshape(64, 512), weights[:, pl.ds(start, 512)], NT, preferred_element_type=jnp.float32
+            term = jnp.dot(
+                near[buf, c].reshape(64, 512), weights[pl.ds(start, 512), :], preferred_element_type=jnp.float32
             )
             acc = term if acc is None else acc + term
         mine[i] = acc[:, :256]
@@ -226,29 +230,40 @@
         col = lax.broadcasted_iota(jnp.int32, (24, 1536), 1)
         tile = lax.broadcasted_iota(jnp.int32, (24, 1536), 0)
         spread = jnp.where(col // TILE == tile, 1.0, 0.0).astype(jnp.bfloat16)
-        flags = jnp.dot(imask_ref[...].astype(jnp.bfloat16), spread, preferred_element_type=jnp.float32)
+        load_imask.wait()
+        flags = jnp.dot(imask[...].astype(jnp.bfloat16), spread, preferred_element_type=jnp.float32)
         where = lax.broadcasted_iota(jnp.int32, (8, 1536), 1) // 512 + me
-        flags = jnp.where((where >= 1) & (where <= 64), flags, 0.0).astype(jnp.bfloat16)
+        flags = jnp.where((where >= 1) & (where <= 64), flags, 0.0)
         load_int.wait()
-        for m in range(8):
-            to = pl.multiple_of(((m % 2 + core) % 2 * 4 + m // 2) * 64, 64)
-            weights[pl.ds(to, 64), :] = raw[m * 64:m * 64 + 64, :] * flags[m:m + 1, :]
+        flag_rows[...] = flags
+        for half in range(2):
+            for pair in range(2):
+                parts = []
+                for k in range(2):
+                    m = 2 * (2 * pair + k) + (core + half) % 2
+                    rows = raw[pl.ds(pl.multiple_of(m * 64, 64), 64), :]
+                    parts.append(rows * flag_rows[pl.ds(m, 1), :].astype(jnp.bfloat16))
+                lanes = slice(half * 256 + pair * 128, half * 256 + pair * 128 + 128)
+                weights[:, lanes] = jnp.concatenate(parts, 0).T
 
     send(0)
     for i in range(2, 8):
         mask_row(i)
     for i in range(1, LEAD):
         send(i)
-    mask_weights()
     stages = (enter, relay, multiply, swap, finish)
     for step in range(8 + LAGS[-1]):
         if step + LEAD < 8:
             send(step + LEAD)
+        if step == 2:
+            mask_weights()
         for stage, lag in zip(stages, LAGS):
             if 0 <= step - lag < 8:
                 stage(step - lag)
 
-    out_ref[...] = total[...].reshape(512, 128).T[:64]
+    out[...] = total[...].reshape(512, 128).T[:64]
+    store = pltpu.make_async_copy(out, out_hbm, mask_sem.at[0])
+    store.start()
 
     def drain(ref, sem):
         pltpu.make_async_copy(ref, ref, sem).wait()
@@ -276,6 +291,7 @@
 
     drain(other, core_send.at[0])
     drain(from_x, x_send.at[0])
+    store.wait()
 
 
 def body(amplitudes, integrals, amplitude_mask, integral_mask):
@@ -287,14 +303,18 @@
         in_specs=[
             pl.BlockSpec(memory_space=pl.ANY),
             pl.BlockSpec(memory_space=pl.ANY),
-            pl.BlockSpec(memory_space=pltpu.VMEM),
-            pl.BlockSpec(memory_space=pltpu.VMEM),
+            pl.BlockSpec(memory_space=pl.ANY),
+            pl.BlockSpec(memory_space=pl.ANY),
         ],
-        out_specs=pl.BlockSpec(memory_space=pltpu.VMEM),
+        out_specs=pl.BlockSpec(memory_space=pl.ANY),
         scratch_shapes=[
+            pltpu.VMEM((64, 512), f32),
+            pltpu.VMEM((1, 512), jnp.int32),
+            pltpu.VMEM((8, 24), jnp.int32),
+            pltpu.VMEM((8, 1536), f32),
             pltpu.VMEM((64, 8, 512), bf16),
             pltpu.VMEM((512, 1536), bf16),
-            pltpu.VMEM((512, 1536), bf16),
+            pltpu.VMEM((1536, 512), bf16),
             pltpu.VMEM((64, 8, 512), bf16),
             pltpu.VMEM((64, 8, 512), bf16),
             pltpu.VMEM((4, 8, 8, 8, 512), bf16),
@@ -305,6 +325,7 @@
             pltpu.VMEM((8, 3, 32, 128), f32),
             pltpu.VMEM((64, 8, 128), f32),
             pltpu.SemaphoreType.REGULAR((8,)),
+            dma((2,)),
             dma((8,)),
             dma((1,)),
             dma((1,)),

time: 51.6 us -> 50.3 us (0.975)
  Pallas kernels: 49.8 us -> 48.5 us
    pallas_call x1, Pallas kernels: 49.8 us -> 48.5 us  [body(): pl.pallas_call(kernel, out_shape=jax.ShapeDtypeStruct((64, 512), f32), in...]
where the time goes in v5:
time: 50.3 us; the launch traced here: 50.1 us
  Pallas kernels  48.5 us (96%)
  local copies, waits for them, and re-layouts  1.57 us (3%)
    pallas_call x1, Pallas kernels, body(): pl.pallas_call(kernel, out_shape=jax.ShapeDtypeStruct((64, 512), f32), in...  48.5 us
    unnamed x1, local copies, waits for them, and re-layouts  1.57 us

profile of v5, /device:TPU:8, one launch (start us, length us, event | category | flops | bytes accessed | tf_op | source)
XLA Modules:
  0.0 50.1 jit_solution(1412430952519082969)
XLA Ops:
  0.0 48.5 %ladder.1 = f32[64,512]{1,0:T(8,128)} custom-call(bf16[64,8,512]{2,1,0:T(8,128)(2,1)} %bitcast.7, bf16[512,1536]{1,0:T(8,128)(2,1)} %bitcast.6, s32[1,512]{1,0:T(1,128)} %bitcast.9, s32[8,24]{1,0:T(8,128)} %bitcast.8), custom_call_target="tpu_custom_call" | custom-call | tf_op jit(solution)/shard_map/ladder/pallas_call | solution.py:300
  48.5 1.6 %copy.6 = f32[64,512]{1,0:T(8,128)} copy(f32[64,512]{1,0:T(8,128)} %ladder.1) | data formatting | bytes 262144

commit v6 on v5

--- a/solution.py
+++ b/solution.py
@@ -91,7 +91,7 @@
         to_y = (y + 8 - OFFSETS[i]) % 8
         if i > 0:
             pl.semaphore_wait(row_in.at[to_y], 1)
-        for rel in (0, 1, 7, 2, 6, 3, 5, 4):
+        for rel in (4, 3, 5, 2, 6, 1, 7, 0):
             to_z = (z + 8 + turn * rel) % 8
             if rel == 0:
                 to, buf, spot, group = to_z, HERE, 0, HERE_SELF

time: 50.3 us -> 50.1 us (level)
  no operation moved by 1% of the time
where the time goes in v6:
time: 50.1 us; the launch traced here: 50 us
  Pallas kernels  48.4 us (97%)
  local copies, waits for them, and re-layouts  1.57 us (3%)
    pallas_call x1, Pallas kernels, body(): pl.pallas_call(kernel, out_shape=jax.ShapeDtypeStruct((64, 512), f32), in...  48.4 us
    unnamed x1, local copies, waits for them, and re-layouts  1.57 us

profile of v6, /device:TPU:8, one launch (start us, length us, event | category | flops | bytes accessed | tf_op | source)
XLA Modules:
  0.0 50.0 jit_solution(1879812801958759078)
XLA Ops:
  0.0 48.4 %ladder.1 = f32[64,512]{1,0:T(8,128)} custom-call(bf16[64,8,512]{2,1,0:T(8,128)(2,1)} %bitcast.7, bf16[512,1536]{1,0:T(8,128)(2,1)} %bitcast.6, s32[1,512]{1,0:T(1,128)} %bitcast.9, s32[8,24]{1,0:T(8,128)} %bitcast.8), custom_call_target="tpu_custom_call" | custom-call | tf_op jit(solution)/shard_map/ladder/pallas_call | solution.py:300
  48.4 1.6 %copy.6 = f32[64,512]{1,0:T(8,128)} copy(f32[64,512]{1,0:T(8,128)} %ladder.1) | data formatting | bytes 262144
